TPU v7x, 32 devices: a whole 2x2x4 slice. The times are simulated.
32 devices in a mesh: gx: 4 (over z), gy: 4 (over x, core), gz: 2 (over y).
Axes of the slice: x: 2, y: 2, z: 4, core: 2. Of those that a mesh axis runs over, the one named last changes fastest.
Arguments:
- coefficients: bfloat16 [8, 32, 32, 16, 256], P(None, 'gx', 'gy', 'gz'), may hold values from -6 to 6
- fun_count: int32 [4, 4, 2], P('gx', 'gy', 'gz'), may hold values from 64 to 256, as said below
- tile_offset: int32 [4, 4, 2], P('gx', 'gy', 'gz'), may hold values from -1 to 1
- kernel: bfloat16 [4, 256, 256], P('gx'), may hold values from -0.0234375 to 0.0234375
Outputs:
- density: float32 [4, 4, 2, 4096], P('gx', 'gy', 'gz')
Inputs may be any that keep to these rules, and one draw needn't show every extreme that they name: `fun_count`: the slots below a domain's count hold its support functions; the other slots are empty. Some domain has all 256 slots live. `tile_offset`: the kernel tile of a domain is held by the first domain index that differs from its own by the offset, cyclically.
All inputs are finite; a program needn't handle non-finite values.
Results may differ from a plain program's by a relative error of at most 0.007.
Values may be sent and summed in bfloat16 or wider, within the bound.
A program may use at most 64 MiB of HBM per device.

v0:
```python
import jax
import jax.numpy as jnp
from jax import lax
from jax.sharding import PartitionSpec as P

FILT = [0.48296291314453416, 0.8365163037378079, 0.2241438680420134, -0.12940952255126037]
WAVE = [(1.0 if t % 2 == 0 else -1.0) * FILT[3 - t] for t in range(4)]


def with_halo(shard, sides, width):
    for axis, dim in sides:
        count, length = (lax.axis_size(axis), shard.shape[dim])
        up = [(i, (i + 1) % count) for i in range(count - 1)]
        down = [(j, i) for i, j in up]
        last = lax.slice_in_dim(shard, length - width, length, axis=dim)
        initial = lax.slice_in_dim(shard, 0, width, axis=dim)
        before = lax.ppermute(last, axis, up)
        after = lax.ppermute(initial, axis, down)
        shard = jnp.concatenate([before, shard, after], axis=dim)
    return shard


def passed_along(value, axis, steps):
    count = lax.axis_size(axis)
    pairs = [(source, (source + steps) % count) for source in range(count)]
    return lax.ppermute(value, axis, pairs)


def band_table(coarse):
    fine_idx = jnp.arange(2 * coarse, dtype=jnp.int32)[:, None]
    coarse_idx = jnp.arange(coarse + 2, dtype=jnp.int32)[None, :]
    offset = fine_idx - 2 * coarse_idx + 3
    low = jnp.zeros(offset.shape, jnp.float32)
    high = jnp.zeros(offset.shape, jnp.float32)
    for tap in range(4):
        low = low + jnp.where(offset == tap, FILT[tap], 0.0).astype(jnp.float32)
        high = high + jnp.where(offset == tap, WAVE[tap], 0.0).astype(jnp.float32)
    return jnp.stack([low, high])


def body(coefficients, fun_count, tile_offset, kernel):
    high = lax.Precision.HIGHEST
    slots_all = coefficients.shape[4]
    coarse_x = coefficients.shape[1]
    coarse_y = coefficients.shape[2]
    coarse_z = coefficients.shape[3]
    live_count = fun_count.reshape(())
    slots = jnp.arange(slots_all, dtype=jnp.int32)
    live = jnp.where(
        (slots < live_count)[None, None, None, None, :], coefficients, jnp.zeros((), jnp.bfloat16)
    )
    extended = with_halo(live, (("gx", 1),), 1)
    data = extended.astype(jnp.float32)
    data = data.reshape((2, 4) + data.shape[1:])
    after_x = jnp.einsum("cnk,cpkyzf->pnyzf", band_table(coarse_x), data, precision=high).astype(
        jnp.bfloat16
    )
    table_y = band_table(coarse_y)
    table_z = band_table(coarse_z)
    extended = with_halo(after_x, (("gy", 2),), 1)
    data = extended.astype(jnp.float32)
    data = data.reshape((2, 2) + data.shape[1:])
    after_y = jnp.einsum("cnk,cpxkzf->pxnzf", table_y, data, precision=high).astype(jnp.bfloat16)
    extended = with_halo(after_y, (("gz", 3),), 1)
    data = extended.astype(jnp.float32)
    phi = jnp.einsum("cnk,cxykf->xynf", table_z, data, precision=high).astype(jnp.bfloat16)
    phi = phi.reshape(-1, slots_all)
    offset = tile_offset.reshape(())
    received = []
    for step_by in (1, -1):
        received.append(passed_along(kernel, "gx", step_by))
    tile = jnp.where(
        offset == -1, received[0][0], jnp.where(offset == 1, received[1][0], kernel[0])
    )
    psi = jnp.dot(phi, tile, preferred_element_type=jnp.float32)
    density = jnp.sum(phi.astype(jnp.float32) * psi, axis=1)
    return density.reshape(1, 1, 1, -1)


def solution(mesh):
    placed = (
        P(None, "gx", "gy", "gz", None),
        P("gx", "gy", "gz"),
        P("gx", "gy", "gz"),
        P("gx", None, None),
    )
    return jax.shard_map(
        body, mesh=mesh, in_specs=placed, out_specs=P("gx", "gy", "gz", None), check_vma=False
    )
```

profile of v0, /device:TPU:1, one launch (start us, length us, event | category | flops | bytes accessed | tf_op | source)
XLA Modules:
  0.0 57.8 jit_solution(14749791718788286547)
XLA Ops:
  0.7 1.7 %broadcast_select_fusion = bf16[8,8,8,8,256]{4,3,2,1,0:T(8,128)(2,1)S(1)} fusion(bf16[8,8,8,8,256]{4,3,2,1,0:T(8,128)(2,1)} %param.4, pred[256]{0:T(512)(128)(4,1)S(1)} %iota_compare_fusion), kind=kLoop, calls=%fused_computation.15 | loop fusion | flops 1048576 | bytes 4194560 | tf_op jit(solution)/shard_map/jit(_where)/select_n | solution.py:49
  2.5 4.0 %collective-permute-start = (bf16[8,1,8,8,256]{4,3,2,1,0:T(8,128)(2,1)S(1)}, bf16[8,1,8,8,256]{4,3,2,1,0:T(8,128)(2,1)S(1)}, u32[]{:S(2)}, u32[]{:S(2)}) collective-permute-start(bf16[8,1,8,8,256]{4,3,2,1,0:T(8,128)(2,1)S(1)} %get-tuple-element.9), channel_id=1, source_target_pairs={{0,8},{8,16},{16,24},{1,9},{9,17},{17,25},{2,10},{10,18},{18,26},{... | collective-permute-start | bytes 786440 | tf_op jit(solution)/shard_map/ppermute | solution.py:17
  6.5 1.3 %collective-permute-start.1 = (bf16[8,1,8,8,256]{4,3,2,1,0:T(8,128)(2,1)S(1)}, bf16[8,1,8,8,256]{4,3,2,1,0:T(8,128)(2,1)S(1)}, u32[]{:S(2)}, u32[]{:S(2)}) collective-permute-start(bf16[8,1,8,8,256]{4,3,2,1,0:T(8,128)(2,1)S(1)} %get-tuple-element.10), channel_id=1, source_target_pairs={{8,0},{16,8},{24,16},{9,1},{17,9},{25,17},{10,2},{18,10},{26,18},{... | collective-permute-start | bytes 786440 | tf_op jit(solution)/shard_map/ppermute | solution.py:18
  7.8 3.6 %collective-permute-done = bf16[8,1,8,8,256]{4,3,2,1,0:T(8,128)(2,1)S(1)} collective-permute-done((bf16[8,1,8,8,256]{4,3,2,1,0:T(8,128)(2,1)S(1)}, bf16[8,1,8,8,256]{4,3,2,1,0:T(8,128)(2,1)S(1)}, u32[]{:S(2)}, u32[]{:S(2)}) %collective-permute-start) | collective-permute-done | bytes 262176 | tf_op jit(solution)/shard_map/ppermute | solution.py:17
  11.4 3.8 %collective-permute-done.1 = bf16[8,1,8,8,256]{4,3,2,1,0:T(8,128)(2,1)S(1)} collective-permute-done((bf16[8,1,8,8,256]{4,3,2,1,0:T(8,128)(2,1)S(1)}, bf16[8,1,8,8,256]{4,3,2,1,0:T(8,128)(2,1)S(1)}, u32[]{:S(2)}, u32[]{:S(2)}) %collective-permute-start.1) | collective-permute-done | bytes 262176 | tf_op jit(solution)/shard_map/ppermute | solution.py:18
  15.3 0.3 pad_maximum_fusion
  15.6 3.6 %fusion.6 = bf16[4,16,8,8,256]{4,1,3,2,0:T(8,128)(2,1)S(1)} fusion(bf16[2,4,10,8,8,256]{5,4,3,2,1,0:T(8,128)(2,1)S(1)} %bitcast.43, f32[1,16,10]{2,1,0:T(8,128)S(1)} %get-tuple-element.12, f32[1,16,10]{2,1,0:T(8,128)S(1)} %get-tuple-element.11), kind=kOutput, calls=%fused_computation.13 | convolution fusion | flops 252707136 | bytes 4719872 | tf_op jit(solution)/shard_map/cnk,cpkyzf->pnyzf/dot_general | solution.py:55
  19.2 4.9 %collective-permute-start.2 = (bf16[4,16,1,8,256]{4,1,3,2,0:T(8,128)(2,1)S(1)}, bf16[4,16,1,8,256]{4,1,3,2,0:T(8,128)(2,1)S(1)}, u32[]{:S(2)}, u32[]{:S(2)}) collective-permute-start(bf16[4,16,1,8,256]{4,1,3,2,0:T(8,128)(2,1)S(1)} %get-tuple-element.7), channel_id=1, source_target_pairs={{0,2},{2,4},{4,6},{1,3},{3,5},{5,7},{8,10},{10,12},{12,14},{9,11},... | collective-permute-start | bytes 786440 | tf_op jit(solution)/shard_map/ppermute | solution.py:17
  24.1 1.9 %collective-permute-start.3 = (bf16[4,16,1,8,256]{4,1,3,2,0:T(8,128)(2,1)S(1)}, bf16[4,16,1,8,256]{4,1,3,2,0:T(8,128)(2,1)S(1)}, u32[]{:S(2)}, u32[]{:S(2)}) collective-permute-start(bf16[4,16,1,8,256]{4,1,3,2,0:T(8,128)(2,1)S(1)} %get-tuple-element.8), channel_id=1, source_target_pairs={{2,0},{4,2},{6,4},{3,1},{5,3},{7,5},{10,8},{12,10},{14,12},{11,9},... | collective-permute-start | bytes 786440 | tf_op jit(solution)/shard_map/ppermute | solution.py:18
  26.0 1.4 %collective-permute-done.2 = bf16[4,16,1,8,256]{4,1,3,2,0:T(8,128)(2,1)S(1)} collective-permute-done((bf16[4,16,1,8,256]{4,1,3,2,0:T(8,128)(2,1)S(1)}, bf16[4,16,1,8,256]{4,1,3,2,0:T(8,128)(2,1)S(1)}, u32[]{:S(2)}, u32[]{:S(2)}) %collective-permute-start.2) | collective-permute-done | bytes 262176 | tf_op jit(solution)/shard_map/ppermute | solution.py:17
  27.4 4.4 %collective-permute-done.3 = bf16[4,16,1,8,256]{4,1,3,2,0:T(8,128)(2,1)S(1)} collective-permute-done((bf16[4,16,1,8,256]{4,1,3,2,0:T(8,128)(2,1)S(1)}, bf16[4,16,1,8,256]{4,1,3,2,0:T(8,128)(2,1)S(1)}, u32[]{:S(2)}, u32[]{:S(2)}) %collective-permute-start.3) | collective-permute-done | bytes 262176 | tf_op jit(solution)/shard_map/ppermute | solution.py:18
  31.8 0.3 pad_maximum_fusion.1
  32.1 0.0 copy-start
  32.1 6.5 %fusion.7 = bf16[2,16,16,8,256]{4,2,3,1,0:T(8,128)(2,1)S(1)} fusion(bf16[2,2,16,10,8,256]{5,2,4,3,1,0:T(8,128)(2,1)S(1)} %bitcast.44, f32[1,16,10]{2,1,0:T(8,128)S(1)} %get-tuple-element.12, f32[1,16,10]{2,1,0:T(8,128)S(1)} %get-tuple-element.11), kind=kOutput, calls=%fused_computation.14 | convolution fusion | flops 252707136 | bytes 4719872 | tf_op jit(solution)/shard_map/cnk,cpxkzf->pxnzf/dot_general | solution.py:63
  38.7 3.2 %collective-permute-start.4 = (bf16[2,16,16,1,256]{4,2,3,1,0:T(8,128)(2,1)S(1)}, bf16[2,16,16,1,256]{4,2,3,1,0:T(8,128)(2,1)S(1)}, u32[]{:S(2)}, u32[]{:S(2)}) collective-permute-start(bf16[2,16,16,1,256]{4,2,3,1,0:T(8,128)(2,1)S(1)} %get-tuple-element.5), channel_id=1, source_target_pairs={{0,1},{2,3},{4,5},{6,7},{8,9},{10,11},{12,13},{14,15},{16,17},{18,... | collective-permute-start | bytes 786440 | tf_op jit(solution)/shard_map/ppermute | solution.py:17
  41.9 1.3 %collective-permute-start.5 = (bf16[2,16,16,1,256]{4,2,3,1,0:T(8,128)(2,1)S(1)}, bf16[2,16,16,1,256]{4,2,3,1,0:T(8,128)(2,1)S(1)}, u32[]{:S(2)}, u32[]{:S(2)}) collective-permute-start(bf16[2,16,16,1,256]{4,2,3,1,0:T(8,128)(2,1)S(1)} %get-tuple-element.6), channel_id=1, source_target_pairs={{1,0},{3,2},{5,4},{7,6},{9,8},{11,10},{13,12},{15,14},{17,16},{19,... | collective-permute-start | bytes 786440 | tf_op jit(solution)/shard_map/ppermute | solution.py:18
  43.2 0.0 copy-done
  43.2 1.3 %collective-permute-start.6 = (bf16[1,256,256]{2,1,0:T(8,128)(2,1)S(1)}, bf16[1,256,256]{2,1,0:T(8,128)(2,1)S(1)}, u32[]{:S(2)}, u32[]{:S(2)}) collective-permute-start(bf16[1,256,256]{2,1,0:T(8,128)(2,1)S(1)} %copy-done), channel_id=1, source_target_pairs={{0,8},{8,16},{16,24},{24,0},{1,9},{9,17},{17,25},{25,1},{2,10},{10... | collective-permute-start | bytes 393224 | tf_op jit(solution)/shard_map/ppermute | solution.py:26
  44.6 2.0 %collective-permute-start.7 = (bf16[1,256,256]{2,1,0:T(8,128)(2,1)S(1)}, bf16[1,256,256]{2,1,0:T(8,128)(2,1)S(1)}, u32[]{:S(2)}, u32[]{:S(2)}) collective-permute-start(bf16[1,256,256]{2,1,0:T(8,128)(2,1)S(1)} %copy-done), channel_id=1, source_target_pairs={{0,24},{8,0},{16,8},{24,16},{1,25},{9,1},{17,9},{25,17},{2,26},{10... | collective-permute-start | bytes 393224 | tf_op jit(solution)/shard_map/ppermute | solution.py:26
  47.2 0.0 collective-permute-done.4
  47.2 1.8 %collective-permute-done.5 = bf16[2,16,16,1,256]{4,2,3,1,0:T(8,128)(2,1)S(1)} collective-permute-done((bf16[2,16,16,1,256]{4,2,3,1,0:T(8,128)(2,1)S(1)}, bf16[2,16,16,1,256]{4,2,3,1,0:T(8,128)(2,1)S(1)}, u32[]{:S(2)}, u32[]{:S(2)}) %collective-permute-start.5) | collective-permute-done | bytes 262176 | tf_op jit(solution)/shard_map/ppermute | solution.py:18
  49.0 0.3 pad_maximum_fusion.2
  49.3 2.5 %bitcast_convert_fusion = bf16[16,16,256,16]{2,3,1,0:T(8,128)(2,1)S(1)} fusion(bf16[2,16,16,10,256]{4,2,3,1,0:T(8,128)(2,1)S(1)} %pad_maximum_fusion.2, f32[1,16,10]{2,1,0:T(8,128)S(1)} %get-tuple-element.12, f32[1,16,10]{2,1,0:T(8,128)S(1)} %get-tuple-element.11), kind=kOutput, calls=%fused_computation.1 | convolution fusion | flops 252707136 | bytes 4719872 | tf_op jit(solution)/shard_map/cnk,cxykf->xynf/dot_general | solution.py:66
  51.9 3.0 %copy.11 = bf16[4096,256]{0,1:T(8,128)(2,1)} copy(bf16[4096,256]{1,0:T(8,128)(2,1)S(1)} %bitcast.45) | data formatting | bytes 4194304 | tf_op jit(solution)/shard_map/reshape | solution.py:67
  54.8 0.0 collective-permute-done.6
  54.8 0.0 collective-permute-done.7
  54.8 3.0 %fusion.14 = f32[4096]{0:T(1024)} fusion(bf16[4096,256]{1,0:T(8,128)(2,1)S(1)} %bitcast.46, bf16[4096,256]{0,1:T(8,128)(2,1)} %copy.11, bf16[1,256,256]{2,1,0:T(8,128)(2,1)S(1)} %collective-permute-done.6, bf16[1,256,256]{2,1,0:T(8,128)(2,1)S(1)} %collective-permute-done.7, bf16[1,256,256]{2,1,0:T(8,128)(2,1)S(1)} %copy-done, pred[]{:T(512)} %bitcast.19, ...), kind=kOutput, calls=%fused_computation.16 | convolution fusion | flops 540143616 | bytes 4603906 | tf_op jit(solution)/shard_map/dot_general | solution.py:75
  (6 shorter events, 0.1 us)
Async XLA Ops:
  2.5 9.0 %collective-permute-start = (bf16[8,1,8,8,256]{4,3,2,1,0:T(8,128)(2,1)S(1)}, bf16[8,1,8,8,256]{4,3,2,1,0:T(8,128)(2,1)S(1)}, u32[]{:S(2)}, u32[]{:S(2)}) collective-permute-start(bf16[8,1,8,8,256]{4,3,2,1,0:T(8,128)(2,1)S(1)} %get-tuple-element.9), channel_id=1, source_target_pairs={{0,8},{8,16},{16,24},{1,9},{9,17},{17,25},{2,10},{10,18},{18,26},{... | collective-permute-start | bytes 786440 | tf_op jit(solution)/shard_map/ppermute | solution.py:17
  6.5 8.8 %collective-permute-start.1 = (bf16[8,1,8,8,256]{4,3,2,1,0:T(8,128)(2,1)S(1)}, bf16[8,1,8,8,256]{4,3,2,1,0:T(8,128)(2,1)S(1)}, u32[]{:S(2)}, u32[]{:S(2)}) collective-permute-start(bf16[8,1,8,8,256]{4,3,2,1,0:T(8,128)(2,1)S(1)} %get-tuple-element.10), channel_id=1, source_target_pairs={{8,0},{16,8},{24,16},{9,1},{17,9},{25,17},{10,2},{18,10},{26,18},{... | collective-permute-start | bytes 786440 | tf_op jit(solution)/shard_map/ppermute | solution.py:18
  19.2 8.2 %collective-permute-start.2 = (bf16[4,16,1,8,256]{4,1,3,2,0:T(8,128)(2,1)S(1)}, bf16[4,16,1,8,256]{4,1,3,2,0:T(8,128)(2,1)S(1)}, u32[]{:S(2)}, u32[]{:S(2)}) collective-permute-start(bf16[4,16,1,8,256]{4,1,3,2,0:T(8,128)(2,1)S(1)} %get-tuple-element.7), channel_id=1, source_target_pairs={{0,2},{2,4},{4,6},{1,3},{3,5},{5,7},{8,10},{10,12},{12,14},{9,11},... | collective-permute-start | bytes 786440 | tf_op jit(solution)/shard_map/ppermute | solution.py:17
  24.1 7.7 %collective-permute-start.3 = (bf16[4,16,1,8,256]{4,1,3,2,0:T(8,128)(2,1)S(1)}, bf16[4,16,1,8,256]{4,1,3,2,0:T(8,128)(2,1)S(1)}, u32[]{:S(2)}, u32[]{:S(2)}) collective-permute-start(bf16[4,16,1,8,256]{4,1,3,2,0:T(8,128)(2,1)S(1)} %get-tuple-element.8), channel_id=1, source_target_pairs={{2,0},{4,2},{6,4},{3,1},{5,3},{7,5},{10,8},{12,10},{14,12},{11,9},... | collective-permute-start | bytes 786440 | tf_op jit(solution)/shard_map/ppermute | solution.py:18
  32.1 11.1 %copy-start = (bf16[1,256,256]{2,1,0:T(8,128)(2,1)S(1)}, bf16[1,256,256]{2,1,0:T(8,128)(2,1)}, u32[]{:S(2)}) copy-start(bf16[1,256,256]{2,1,0:T(8,128)(2,1)} %param.7) | copy-start | bytes 393220
  38.7 8.5 %collective-permute-start.4 = (bf16[2,16,16,1,256]{4,2,3,1,0:T(8,128)(2,1)S(1)}, bf16[2,16,16,1,256]{4,2,3,1,0:T(8,128)(2,1)S(1)}, u32[]{:S(2)}, u32[]{:S(2)}) collective-permute-start(bf16[2,16,16,1,256]{4,2,3,1,0:T(8,128)(2,1)S(1)} %get-tuple-element.5), channel_id=1, source_target_pairs={{0,1},{2,3},{4,5},{6,7},{8,9},{10,11},{12,13},{14,15},{16,17},{18,... | collective-permute-start | bytes 786440 | tf_op jit(solution)/shard_map/ppermute | solution.py:17
  41.9 7.1 %collective-permute-start.5 = (bf16[2,16,16,1,256]{4,2,3,1,0:T(8,128)(2,1)S(1)}, bf16[2,16,16,1,256]{4,2,3,1,0:T(8,128)(2,1)S(1)}, u32[]{:S(2)}, u32[]{:S(2)}) collective-permute-start(bf16[2,16,16,1,256]{4,2,3,1,0:T(8,128)(2,1)S(1)} %get-tuple-element.6), channel_id=1, source_target_pairs={{1,0},{3,2},{5,4},{7,6},{9,8},{11,10},{13,12},{15,14},{17,16},{19,... | collective-permute-start | bytes 786440 | tf_op jit(solution)/shard_map/ppermute | solution.py:18
  43.2 11.6 %collective-permute-start.6 = (bf16[1,256,256]{2,1,0:T(8,128)(2,1)S(1)}, bf16[1,256,256]{2,1,0:T(8,128)(2,1)S(1)}, u32[]{:S(2)}, u32[]{:S(2)}) collective-permute-start(bf16[1,256,256]{2,1,0:T(8,128)(2,1)S(1)} %copy-done), channel_id=1, source_target_pairs={{0,8},{8,16},{16,24},{24,0},{1,9},{9,17},{17,25},{25,1},{2,10},{10... | collective-permute-start | bytes 393224 | tf_op jit(solution)/shard_map/ppermute | solution.py:26
  44.6 10.3 %collective-permute-start.7 = (bf16[1,256,256]{2,1,0:T(8,128)(2,1)S(1)}, bf16[1,256,256]{2,1,0:T(8,128)(2,1)S(1)}, u32[]{:S(2)}, u32[]{:S(2)}) collective-permute-start(bf16[1,256,256]{2,1,0:T(8,128)(2,1)S(1)} %copy-done), channel_id=1, source_target_pairs={{0,24},{8,0},{16,8},{24,16},{1,25},{9,1},{17,9},{25,17},{2,26},{10... | collective-permute-start | bytes 393224 | tf_op jit(solution)/shard_map/ppermute | solution.py:26
where the time goes:
time: 58.1 us; the launch traced here: 57.8 us
  starting transfers between devices  19.9 us (34%)
  matrix products  15.6 us (27%)
  waiting for transfers between devices  15 us (26%)
  local copies, waits for them, and re-layouts  3.09 us (5%)
  other arithmetic  2.72 us (5%)
  between operations  1.46 us (3%)
    ppermute x3, starting transfers between devices, with_halo(): before = lax.ppermute(last, axis, up)  12.1 us
    ppermute x3, waiting for transfers between devices, with_halo(): after = lax.ppermute(initial, axis, down)  10 us
    dot_general x1, matrix products, body(): jnp.einsum('cnk,cpxkzf->pxnzf', table_y, data, precision=high)  6.55 us
    ppermute x3, waiting for transfers between devices, with_halo(): before = lax.ppermute(last, axis, up)  4.98 us
    ppermute x3, starting transfers between devices, with_halo(): after = lax.ppermute(initial, axis, down)  4.5 us
    dot_general x1, matrix products, body(): jnp.einsum('cnk,cpkyzf->pnyzf', band_table(coarse_x), data, precision=high)  3.6 us
    ppermute x2, starting transfers between devices, passed_along(): return lax.ppermute(value, axis, pairs)  3.32 us
    dot_general x1, matrix products, body(): psi = jnp.dot(phi, tile, preferred_element_type=jnp.float32)  2.97 us
  transfers between devices with their start and end apart: 8, of which 5 were waited for; matrix products, arithmetic and copies ran while one was open for 10% of the time, Pallas kernels for 0%

commit v1 on v0

v1 whole, which is shorter than its diff:
```python
import jax
import jax.numpy as jnp
import numpy as np
from jax import lax
from jax.experimental import pallas as pl
from jax.experimental.pallas import tpu as pltpu
from jax.sharding import PartitionSpec as P

FILT = [0.48296291314453416, 0.8365163037378079, 0.2241438680420134, -0.12940952255126037]
WAVE = [(1.0 if t % 2 == 0 else -1.0) * FILT[3 - t] for t in range(4)]
BANDS = (FILT, WAVE)
MESH = pl.DeviceIdType.MESH
BF = jnp.bfloat16
F32 = jnp.float32


def synthesis(coarse):
    table = np.zeros((2 * coarse, 2, coarse))
    for n in range(2 * coarse):
        for k in range(coarse):
            t = n - 2 * k + 1
            if 0 <= t < 4:
                for b in range(2):
                    table[n, b, k] = BANDS[b][t]
    return table


def best_scale():
    taps = np.array(FILT)
    prods = (taps[:, None] * taps[None, :]).reshape(-1)
    scales = np.linspace(1.0, 2.0, 4001)
    scaled = scales[:, None] * prods[None, :]
    rounded = scaled.astype(jnp.bfloat16).astype(np.float64)
    errors = np.sum(((rounded - scaled) / scales[:, None]) ** 2, axis=1)
    return float(scales[int(np.argmin(errors))])


def tables(cy, cz, scale):
    sy, sz = synthesis(cy), synthesis(cz)
    ny, nz = 2 * cy, 2 * cz
    rows = 4 * cy * cz
    own = np.einsum("ybk,zcl->zybckl", sy, sz).reshape(ny * nz, rows)
    halo = np.zeros((nz, ny, 2, 2, cz))
    halo[:, 0, 0] = sz
    halo[:, ny - 1, 1] = sz
    send_y = np.zeros((2, 2, cz, 2, 2, cy, cz))
    send_z = np.zeros((2, ny, 2, 2, cy, cz))
    send_zh = np.zeros((2, ny, 2, 2, cz))
    for b in range(2):
        for c in range(2):
            for l in range(cz):
                send_y[0, c, l, b, c, cy - 1, l] = BANDS[b][3]
                send_y[1, c, l, b, c, 0, l] = BANDS[b][0]
            send_z[0, :, b, c, :, cz - 1] = sy[:, b] * BANDS[c][3]
            send_z[1, :, b, c, :, 0] = sy[:, b] * BANDS[c][0]
    for c in range(2):
        for side, row in ((0, 0), (1, ny - 1)):
            send_zh[0, row, side, c, cz - 1] = BANDS[c][3]
            send_zh[1, row, side, c, 0] = BANDS[c][0]
    wide = lambda a, r: a.reshape(r, -1)
    main = np.concatenate([scale * own, wide(send_y, 4 * cz), scale * wide(send_z, 2 * ny)], 0)
    small = np.concatenate([wide(halo, ny * nz), wide(send_zh, 2 * ny)], 0) * scale
    return main.astype(jnp.bfloat16), small.astype(jnp.bfloat16)


def rowsum(prod):
    width = prod.shape[1] // 2
    half = prod[:, :width] + prod[:, width:]
    return jnp.sum(half.T, axis=0, keepdims=True)


def make_kernel(cx, cy, cz, slots, scale):
    fx, fy, fz = 2 * cx, 2 * cy, 2 * cz
    face = cy * cz
    cells = fy * fz
    rows = 4 * face
    inv = 1.0 / (scale * scale)

    def kernel(coef, cnt, off, ktile, main_h, small_h, den, denb,
               cv, ax, main, small, xo, xi, yo, yi, zo, zi, zb, tiles, tile, lsem, ssem, rsem):
        ix, iy, iz = lax.axis_index("gx"), lax.axis_index("gy"), lax.axis_index("gz")
        gx, gy, gz = lax.axis_size("gx"), lax.axis_size("gy"), lax.axis_size("gz")
        index = {"gx": ix, "gy": iy, "gz": iz}
        size = {"gx": gx, "gy": gy, "gz": gz}

        def local(i, src, dst):
            return pltpu.make_async_copy(src, dst, lsem.at[i])

        loads = [
            local(0, coef.at[:, 0], cv.at[:, 0]),
            local(1, coef.at[:, cx - 1], cv.at[:, cx - 1]),
            local(2, coef.at[:, pl.ds(1, cx - 2)], cv.at[:, pl.ds(1, cx - 2)]),
            local(3, main_h, main),
            local(4, small_h, small),
            local(5, ktile.at[0], tiles.at[2]),
        ]
        for load in loads:
            load.start()

        def has(axis, step):
            return index[axis] < size[axis] - 1 if step > 0 else index[axis] > 0

        barrier = pltpu.get_barrier_semaphore()
        ring = {1: lax.rem(ix + 1, gx), -1: lax.rem(ix + gx - 1, gx)}
        for step in (1, -1):
            pl.semaphore_signal(barrier, inc=1, device_id={"gx": ring[step]}, device_id_type=MESH)
            for axis in ("gy", "gz"):
                @pl.when(has(axis, step))
                def _():
                    pl.semaphore_signal(
                        barrier, inc=1, device_id={axis: index[axis] + step}, device_id_type=MESH
                    )

        def remote(i, src, dst, axis, target):
            return pltpu.make_async_remote_copy(
                src_ref=src, dst_ref=dst, send_sem=ssem.at[i], recv_sem=rsem.at[i],
                device_id={axis: target}, device_id_type=MESH,
            )

        early, late = pl.ds(2, fx - 2), pl.ds(0, 2)
        up, dn = 0, 1
        copies = {}
        for side, step in ((up, 1), (dn, -1)):
            copies["x", side] = (remote(side, xo.at[side], xi.at[side], "gx", ix + step), "gx", step)
            for part, (name, planes) in enumerate((("e", early), ("l", late))):
                copies["y" + name, side] = (
                    remote(4 + 2 * part + side, yo.at[side, planes],
                           yi.at[planes, pl.ds(side * 2 * cz, 2 * cz)], "gy", iy + step),
                    "gy", step)
                copies["z" + name, side] = (
                    remote(8 + 2 * part + side, zo.at[side, planes], zi.at[side, planes], "gz", iz + step),
                    "gz", step)
        rings = [remote(2 + side, ktile.at[0], tiles.at[side], "gx", ring[step])
                 for side, step in ((up, 1), (dn, -1))]

        def start(key):
            copy, axis, step = copies[key]
            pl.when(has(axis, step))(lambda: copy.start())

        def arrive(key):
            copy, axis, step = copies[key]
            pl.when(has(axis, -step))(lambda: copy.wait_recv())

        @pl.when(ix == 0)
        def _():
            xi[0] = jnp.zeros(xi.shape[1:], BF)

        @pl.when(ix == gx - 1)
        def _():
            xi[1] = jnp.zeros(xi.shape[1:], BF)

        @pl.when(iy == 0)
        def _():
            yi[:, 0 : 2 * cz] = jnp.zeros((fx, 2 * cz, slots), BF)

        @pl.when(iy == gy - 1)
        def _():
            yi[:, 2 * cz : 4 * cz] = jnp.zeros((fx, 2 * cz, slots), BF)

        @pl.when(iz == 0)
        def _():
            zi[0] = jnp.zeros(zi.shape[1:], BF)

        @pl.when(iz == gz - 1)
        def _():
            zi[1] = jnp.zeros(zi.shape[1:], BF)

        live = jnp.where(
            lax.broadcasted_iota(jnp.int32, (1, slots), 1) < cnt[0, 0, 0], 1.0, 0.0
        ).astype(F32)
        low = [FILT[t] * live for t in range(4)]
        high = [WAVE[t] * live for t in range(4)]

        def bands(k, p):
            return cv[p, k].astype(F32), cv[4 + p, k].astype(F32)

        def block(p):
            return pl.ds(p * face, face)

        loads[0].wait()
        for p in range(4):
            s, w = bands(0, p)
            xo[dn, block(p)] = (low[0] * s + high[0] * w).astype(BF)
        loads[1].wait()
        for p in range(4):
            s, w = bands(cx - 1, p)
            xo[up, block(p)] = (low[3] * s + high[3] * w).astype(BF)
        peers = 2
        for axis in ("gy", "gz"):
            i, n = index[axis], size[axis]
            peers = peers + (i + n - 1) // n + ((i + 1) % n + n - 1) // n
        pl.semaphore_wait(barrier, peers)
        start(("x", dn))
        start(("x", up))
        for copy in rings:
            copy.start()

        loads[2].wait()

        @pl.loop(1, cx)
        def _(m):
            for p in range(4):
                s0, w0 = bands(m - 1, p)
                s1, w1 = bands(m, p)
                ax[2 * m, block(p)] = (
                    low[2] * s0 + high[2] * w0 + low[0] * s1 + high[0] * w1
                ).astype(BF)
                ax[2 * m + 1, block(p)] = (
                    low[1] * s1 + high[1] * w1 + low[3] * s0 + high[3] * w0
                ).astype(BF)

        loads[3].wait()
        half = 2 * cz

        def send_y(q):
            out = jnp.dot(main[pl.ds(cells, 2 * half), :], ax[q], preferred_element_type=F32)
            yo[up, q] = out[:half].astype(BF)
            yo[dn, q] = out[half:].astype(BF)

        pl.loop(2, fx)(send_y)
        start(("ye", up))
        start(("ye", dn))

        arrive(("x", up))
        arrive(("x", dn))
        for p in range(4):
            s, w = bands(cx - 1, p)
            ax[0, block(p)] = (low[2] * s + high[2] * w + xi[dn, block(p)].astype(F32)).astype(BF)
            s, w = bands(0, p)
            ax[1, block(p)] = (low[1] * s + high[1] * w + xi[up, block(p)].astype(F32)).astype(BF)
        pl.loop(0, 2)(send_y)
        start(("yl", up))
        start(("yl", dn))

        loads[4].wait()

        def send_z(q):
            out = jnp.dot(main[pl.ds(cells + 2 * half, 2 * fy), :], ax[q], preferred_element_type=F32)
            out += jnp.dot(small[pl.ds(cells, 2 * fy), :], yi[q], preferred_element_type=F32)
            zo[up, q] = out[:fy].astype(BF)
            zo[dn, q] = out[fy:].astype(BF)

        arrive(("ye", up))
        arrive(("ye", dn))
        pl.loop(2, fx)(send_z)
        start(("ze", up))
        start(("ze", dn))
        arrive(("yl", up))
        arrive(("yl", dn))
        pl.loop(0, 2)(send_z)
        start(("zl", up))
        start(("zl", dn))

        loads[5].wait()
        for copy in rings:
            copy.wait_recv()
        away = off[0, 0, 0]
        before = jnp.where(away == -1, 1.0, 0.0).astype(F32)
        after = jnp.where(away == 1, 1.0, 0.0).astype(F32)
        here = 1.0 - before - after
        tile[...] = (
            tiles[up].astype(F32) * before + tiles[dn].astype(F32) * after
            + tiles[2].astype(F32) * here
        ).astype(BF)

        @pl.loop(0, fx)
        def _(q):
            pre = jnp.dot(main[pl.ds(0, cells), :], ax[q], preferred_element_type=F32)
            pre += jnp.dot(small[pl.ds(0, cells), :], yi[q], preferred_element_type=F32)
            zb[0, q] = pre[:fy]
            zb[1, q] = pre[cells - fy :]
            phi = pre.astype(BF)
            psi = jnp.dot(phi, tile[...], preferred_element_type=F32)
            den[pl.ds(q, 1), :] = rowsum(phi.astype(F32) * psi) * inv

        for key in (("ze", up), ("ze", dn), ("zl", up), ("zl", dn)):
            arrive(key)
        for side in range(2):
            pre = zb[side] + zi[side].astype(F32)
            phi = pre.reshape(fx * fy, slots).astype(BF)
            psi = jnp.dot(phi, tile[...], preferred_element_type=F32)
            denb[pl.ds(side, 1), :] = rowsum(phi.astype(F32) * psi) * inv

        for copy, axis, step in copies.values():
            pl.when(has(axis, step))(lambda copy=copy: copy.wait_send())
        for copy in rings:
            copy.wait_send()

    return kernel


def body(coefficients, fun_count, tile_offset, kernel):
    bands, cx, cy, cz, slots = coefficients.shape
    fx, fy, fz = 2 * cx, 2 * cy, 2 * cz
    cells, rows = fy * fz, 4 * cy * cz
    scale = best_scale()
    main, small = tables(cy, cz, scale)
    anywhere = pl.BlockSpec(memory_space=pl.ANY)
    scalar = pl.BlockSpec(memory_space=pltpu.SMEM)
    vmem = pl.BlockSpec(memory_space=pltpu.VMEM)
    den, denb = pl.pallas_call(
        make_kernel(cx, cy, cz, slots, scale),
        out_shape=(
            jax.ShapeDtypeStruct((fx, cells), F32),
            jax.ShapeDtypeStruct((2, fx * fy), F32),
        ),
        in_specs=[anywhere, scalar, scalar, anywhere, anywhere, anywhere],
        out_specs=(vmem, vmem),
        scratch_shapes=[
            pltpu.VMEM((bands, cx, cy * cz, slots), BF),
            pltpu.VMEM((fx, rows, slots), BF),
            pltpu.VMEM(main.shape, BF),
            pltpu.VMEM(small.shape, BF),
            pltpu.VMEM((2, rows, slots), BF),
            pltpu.VMEM((2, rows, slots), BF),
            pltpu.VMEM((2, fx, 2 * cz, slots), BF),
            pltpu.VMEM((fx, 4 * cz, slots), BF),
            pltpu.VMEM((2, fx, fy, slots), BF),
            pltpu.VMEM((2, fx, fy, slots), BF),
            pltpu.VMEM((2, fx, fy, slots), F32),
            pltpu.VMEM((3, slots, slots), BF),
            pltpu.VMEM((slots, slots), BF),
            pltpu.SemaphoreType.DMA((6,)),
            pltpu.SemaphoreType.DMA((12,)),
            pltpu.SemaphoreType.DMA((12,)),
        ],
        compiler_params=pltpu.CompilerParams(
            collective_id=0, has_side_effects=True, vmem_limit_bytes=40 * 2**20
        ),
    )(
        coefficients.reshape(bands, cx, cy * cz, slots),
        fun_count, tile_offset, kernel, jnp.asarray(main), jnp.asarray(small),
    )
    den = jnp.roll(den, -1, axis=0).reshape(fx, fz, fy)
    faces = jnp.roll(denb.reshape(2, fx, fy), -1, axis=1)
    den = jnp.concatenate([faces[0][:, None], den[:, 1:-1], faces[1][:, None]], axis=1)
    return den.transpose(0, 2, 1).reshape(1, 1, 1, -1)


def solution(mesh):
    placed = (
        P(None, "gx", "gy", "gz", None),
        P("gx", "gy", "gz"),
        P("gx", "gy", "gz"),
        P("gx", None, None),
    )
    return jax.shard_map(
        body, mesh=mesh, in_specs=placed, out_specs=P("gx", "gy", "gz", None), check_vma=False
    )
```

time: 58.1 us -> 30.6 us (0.53)
  Pallas kernels: 0 us -> 23.6 us
  starting transfers between devices: 19.9 us -> 0 us
  matrix products: 15.6 us -> 0 us
  waiting for transfers between devices: 15 us -> 0 us
  other arithmetic: 2.72 us -> 0.06 us
  local copies, waits for them, and re-layouts: 3.09 us -> 5.3 us
    pallas_call x0 -> x1, Pallas kernels: none -> 23.6 us  [body(): pl.pallas_call(make_kernel(cx, cy, cz, slots, scale), out_shape=(jax.Shap...]
    ppermute x8 -> x0, starting transfers between devices: 19.9 us -> none  [the longest x3 12.1 us: with_halo(): before = lax.ppermute(last, axis, up)]
    dot_general x4 -> x0, matrix products: 15.6 us -> none  [the longest x1 6.55 us: body(): jnp.einsum('cnk,cpxkzf->pxnzf', table_y, data, precision=high)]
    ppermute x8 -> x0, waiting for transfers between devices: 15 us -> none  [the longest x3 10 us: with_halo(): after = lax.ppermute(initial, axis, down)]
    unnamed x2 -> x8, local copies, waits for them, and re-layouts: 0.01 us -> 4.29 us
    reshape x1 -> x3, local copies, waits for them, and re-layouts: 2.96 us -> 0.89 us  [the longest x1 0.72 us: body(): return den.transpose(0, 2, 1).reshape(1, 1, 1, -1)]
    select_n x1 -> x0, other arithmetic: 1.73 us -> none  [body(): jnp.where((slots < live_count)[None, None, None, None, :], coefficients,...]
    concatenate x3 -> x2, other arithmetic: 0.96 us -> 0.02 us  [the longest x1 0.01 us: body(): faces = jnp.roll(denb.reshape(2, fx, fy), -1, axis=1)]
  transfers between devices with their start and end apart: 8 -> 0, of which waited for: 5 -> 0; matrix products, arithmetic and copies ran while one was open for 10% -> 0% of each run, Pallas kernels for 0% -> 0%
where the time goes in v1:
time: 30.6 us; the launch traced here: 30.3 us
  Pallas kernels  23.6 us (77%)
  local copies, waits for them, and re-layouts  5.3 us (17%)
  between operations  1.38 us (5%)
    pallas_call x1, Pallas kernels, body(): pl.pallas_call(make_kernel(cx, cy, cz, slots, scale), out_shape=(jax.Shap...  23.6 us
    unnamed x8, local copies, waits for them, and re-layouts  4.29 us
    reshape x1, local copies, waits for them, and re-layouts, body(): return den.transpose(0, 2, 1).reshape(1, 1, 1, -1)  0.72 us

profile of v1, /device:TPU:1, one launch (start us, length us, event | category | flops | bytes accessed | tf_op | source)
XLA Modules:
  0.0 30.3 jit_solution(3049621811917803561)
XLA Ops:
  1.3 0.0 copy-start
  1.3 1.6 %copy-done = bf16[8,8,8,8,256]{4,3,2,1,0:T(8,128)(2,1)S(1)} copy-done((bf16[8,8,8,8,256]{4,3,2,1,0:T(8,128)(2,1)S(1)}, bf16[8,8,8,8,256]{4,3,2,1,0:T(8,128)(2,1)}, u32[]{:S(2)}) %copy-start) | copy-done | bytes 2097176
  2.9 0.0 copy-start.1
  2.9 0.9 %copy-done.1 = bf16[320,256]{1,0:T(8,128)(2,1)S(1)} copy-done((bf16[320,256]{1,0:T(8,128)(2,1)S(1)}, bf16[320,256]{1,0:T(8,128)(2,1)}, u32[]{:S(2)}) %copy-start.1) | copy-done | bytes 163864
  3.8 0.0 copy-start.2
  3.8 0.9 %copy-done.2 = bf16[1,256,256]{2,1,0:T(8,128)(2,1)S(1)} copy-done((bf16[1,256,256]{2,1,0:T(8,128)(2,1)S(1)}, bf16[1,256,256]{2,1,0:T(8,128)(2,1)}, u32[]{:S(2)}) %copy-start.2) | copy-done | bytes 131096
  4.7 0.0 copy-start.3
  4.7 0.9 %copy-done.3 = bf16[288,32]{1,0:T(8,128)(2,1)S(1)} copy-done((bf16[288,32]{1,0:T(8,128)(2,1)S(1)}, bf16[288,32]{1,0:T(8,128)(2,1)}, u32[]{:S(2)}) %copy-start.3) | copy-done | bytes 18456
  5.6 23.6 %shard_map.64 = (f32[16,256]{1,0:T(8,128)S(1)}, f32[2,256]{1,0:T(2,128)S(1)}) custom-call(bf16[8,8,64,256]{3,2,1,0:T(8,128)(2,1)S(1)} %bitcast.9, s32[1,1,1]{2,1,0:T(1,128)S(6)} %copy.10.cnt, s32[1,1,1]{2,1,0:T(1,128)S(6)} %copy.11.off, bf16[1,256,256]{2,1,0:T(8,128)(2,1)S(1)} %copy-done.2, bf16[320,256]{1,0:T(8,128)(2,1)S(1)} %copy-done.1, ...), custom_call_target="tpu_custom_call" | custom-call | tf_op jit(solution)/shard_map/pallas_call | solution.py:301
  29.2 0.1 reshape.13
  29.3 0.1 reshape.14
  29.5 0.1 copy.9
  29.6 0.7 %reshape.15 = f32[1,1,1,4096]{3,2,1,0:T(1,128)} reshape(f32[16,16,16]{2,1,0:T(8,128)S(1)} %copy.9) | data formatting | bytes 32768 | tf_op jit(solution)/shard_map/reshape | solution.py:337
  (8 shorter events, 0.1 us)
Async XLA Ops:
  1.3 1.6 %copy-start = (bf16[8,8,8,8,256]{4,3,2,1,0:T(8,128)(2,1)S(1)}, bf16[8,8,8,8,256]{4,3,2,1,0:T(8,128)(2,1)}, u32[]{:S(2)}) copy-start(bf16[8,8,8,8,256]{4,3,2,1,0:T(8,128)(2,1)} %param.6) | copy-start | bytes 6291460
  2.9 0.9 %copy-start.1 = (bf16[320,256]{1,0:T(8,128)(2,1)S(1)}, bf16[320,256]{1,0:T(8,128)(2,1)}, u32[]{:S(2)}) copy-start(bf16[320,256]{1,0:T(8,128)(2,1)} %constant.4.clone.main_h) | copy-start | bytes 491524
  3.8 0.9 %copy-start.2 = (bf16[1,256,256]{2,1,0:T(8,128)(2,1)S(1)}, bf16[1,256,256]{2,1,0:T(8,128)(2,1)}, u32[]{:S(2)}) copy-start(bf16[1,256,256]{2,1,0:T(8,128)(2,1)} %ktile.1) | copy-start | bytes 393220
  4.7 0.9 %copy-start.3 = (bf16[288,32]{1,0:T(8,128)(2,1)S(1)}, bf16[288,32]{1,0:T(8,128)(2,1)}, u32[]{:S(2)}) copy-start(bf16[288,32]{1,0:T(8,128)(2,1)} %constant.5.clone.small_h) | copy-start | bytes 55300

commit v2 on v1

--- a/solution.py
+++ b/solution.py
@@ -35,32 +35,41 @@
     return float(scales[int(np.argmin(errors))])
 
 
+def cell_order(fy, fz):
+    z_faces = [(z, y) for z in (0, fz - 1) for y in range(fy)]
+    y_faces = [(z, y) for y in (0, fy - 1) for z in range(1, fz - 1)]
+    inner = [(z, y) for z in range(1, fz - 1) for y in range(1, fy - 1)]
+    fill = -len(y_faces) % 16
+    y_faces, inner = y_faces + inner[:fill], inner[fill:]
+    return inner + y_faces + z_faces, len(inner), len(y_faces), len(z_faces)
+
+
 def tables(cy, cz, scale):
     sy, sz = synthesis(cy), synthesis(cz)
-    ny, nz = 2 * cy, 2 * cz
+    fy, fz = 2 * cy, 2 * cz
     rows = 4 * cy * cz
-    own = np.einsum("ybk,zcl->zybckl", sy, sz).reshape(ny * nz, rows)
-    halo = np.zeros((nz, ny, 2, 2, cz))
+    order, inner, y_rows, z_rows = cell_order(fy, fz)
+    pick = np.array([z * fy + y for z, y in order])
+    own = np.einsum("ybk,zcl->zybckl", sy, sz).reshape(fy * fz, rows)[pick]
+    halo = np.zeros((fz, fy, 2, 2, cz))
     halo[:, 0, 0] = sz
-    halo[:, ny - 1, 1] = sz
-    send_y = np.zeros((2, 2, cz, 2, 2, cy, cz))
-    send_z = np.zeros((2, ny, 2, 2, cy, cz))
-    send_zh = np.zeros((2, ny, 2, 2, cz))
-    for b in range(2):
-        for c in range(2):
-            for l in range(cz):
-                send_y[0, c, l, b, c, cy - 1, l] = BANDS[b][3]
-                send_y[1, c, l, b, c, 0, l] = BANDS[b][0]
+    halo[:, fy - 1, 1] = sz
+    halo = halo.reshape(fy * fz, 4 * cz)[pick]
+    send_z = np.zeros((2, fy, 2, 2, cy, cz))
+    send_zh = np.zeros((2, fy, 2, 2, cz))
+    for c in range(2):
+        for b in range(2):
             send_z[0, :, b, c, :, cz - 1] = sy[:, b] * BANDS[c][3]
             send_z[1, :, b, c, :, 0] = sy[:, b] * BANDS[c][0]
-    for c in range(2):
-        for side, row in ((0, 0), (1, ny - 1)):
+        for side, row in ((0, 0), (1, fy - 1)):
             send_zh[0, row, side, c, cz - 1] = BANDS[c][3]
             send_zh[1, row, side, c, 0] = BANDS[c][0]
-    wide = lambda a, r: a.reshape(r, -1)
-    main = np.concatenate([scale * own, wide(send_y, 4 * cz), scale * wide(send_z, 2 * ny)], 0)
-    small = np.concatenate([wide(halo, ny * nz), wide(send_zh, 2 * ny)], 0) * scale
-    return main.astype(jnp.bfloat16), small.astype(jnp.bfloat16)
+    main = scale * np.concatenate([own, send_z.reshape(2 * fy, rows)], 0)
+    small = scale * np.concatenate([halo[inner:], send_zh.reshape(2 * fy, 4 * cz)], 0)
+    back = np.zeros((fy * fz, fy * fz))
+    for at, (z, y) in enumerate(order):
+        back[at, y * fz + z] = 1.0
+    return [t.astype(jnp.bfloat16) for t in (main, small, back)]
 
 
 def rowsum(prod):
@@ -75,9 +84,12 @@
     cells = fy * fz
     rows = 4 * face
     inv = 1.0 / (scale * scale)
-
-    def kernel(coef, cnt, off, ktile, main_h, small_h, den, denb,
-               cv, ax, main, small, xo, xi, yo, yi, zo, zi, zb, tiles, tile, lsem, ssem, rsem):
+    _, inner, y_rows, z_rows = cell_order(fy, fz)
+    edge = y_rows + z_rows
+
+    def kernel(coef, cnt, off, ktile, main_h, small_h, back_h, den,
+               cv, ax, main, small, back, xo, xi, yo, yi, zo, zi, phis, edges, den_in, den_ed,
+               tiles, tile, lsem, ssem, rsem):
         ix, iy, iz = lax.axis_index("gx"), lax.axis_index("gy"), lax.axis_index("gz")
         gx, gy, gz = lax.axis_size("gx"), lax.axis_size("gy"), lax.axis_size("gz")
         index = {"gx": ix, "gy": iy, "gz": iz}
@@ -93,6 +105,7 @@
             local(3, main_h, main),
             local(4, small_h, small),
             local(5, ktile.at[0], tiles.at[2]),
+            local(6, back_h, back),
         ]
         for load in loads:
             load.start()
@@ -197,6 +210,15 @@
 
         loads[2].wait()
 
+        def send_y(q):
+            for side, tap, k in ((up, 3, cy - 1), (dn, 0, 0)):
+                parts = []
+                for c in range(2):
+                    s = ax[q, pl.ds(c * face + k * cz, cz)].astype(F32)
+                    w = ax[q, pl.ds((2 + c) * face + k * cz, cz)].astype(F32)
+                    parts.append(FILT[tap] * s + WAVE[tap] * w)
+                yo[side, q] = jnp.concatenate(parts, axis=0).astype(BF)
+
         @pl.loop(1, cx)
         def _(m):
             for p in range(4):
@@ -208,18 +230,21 @@
                 ax[2 * m + 1, block(p)] = (
                     low[1] * s1 + high[1] * w1 + low[3] * s0 + high[3] * w0
                 ).astype(BF)
-
-        loads[3].wait()
-        half = 2 * cz
-
-        def send_y(q):
-            out = jnp.dot(main[pl.ds(cells, 2 * half), :], ax[q], preferred_element_type=F32)
-            yo[up, q] = out[:half].astype(BF)
-            yo[dn, q] = out[half:].astype(BF)
-
-        pl.loop(2, fx)(send_y)
+            send_y(2 * m)
+            send_y(2 * m + 1)
+
         start(("ye", up))
         start(("ye", dn))
+        loads[3].wait()
+        loads[4].wait()
+
+        def own_cells(q):
+            pre = jnp.dot(main[...], ax[q], preferred_element_type=F32)
+            phis[q] = pre[:inner].astype(BF)
+            edges[q] = pre[inner:]
+
+        for q in range(2, fx):
+            own_cells(q)
 
         arrive(("x", up))
         arrive(("x", dn))
@@ -228,30 +253,34 @@
             ax[0, block(p)] = (low[2] * s + high[2] * w + xi[dn, block(p)].astype(F32)).astype(BF)
             s, w = bands(0, p)
             ax[1, block(p)] = (low[1] * s + high[1] * w + xi[up, block(p)].astype(F32)).astype(BF)
-        pl.loop(0, 2)(send_y)
+        send_y(0)
+        send_y(1)
         start(("yl", up))
         start(("yl", dn))
 
-        loads[4].wait()
-
-        def send_z(q):
-            out = jnp.dot(main[pl.ds(cells + 2 * half, 2 * fy), :], ax[q], preferred_element_type=F32)
-            out += jnp.dot(small[pl.ds(cells, 2 * fy), :], yi[q], preferred_element_type=F32)
-            zo[up, q] = out[:fy].astype(BF)
-            zo[dn, q] = out[fy:].astype(BF)
+        def y_halo(q):
+            pre = edges[q] + jnp.dot(small[...], yi[q], preferred_element_type=F32)
+            edges[q, :edge] = pre[:edge]
+            zo[up, q] = pre[edge : edge + fy].astype(BF)
+            zo[dn, q] = pre[edge + fy :].astype(BF)
 
         arrive(("ye", up))
         arrive(("ye", dn))
-        pl.loop(2, fx)(send_z)
+        for q in range(2, fx):
+            y_halo(q)
         start(("ze", up))
         start(("ze", dn))
+        own_cells(0)
+        own_cells(1)
         arrive(("yl", up))
         arrive(("yl", dn))
-        pl.loop(0, 2)(send_z)
+        y_halo(0)
+        y_halo(1)
         start(("zl", up))
         start(("zl", dn))
 
         loads[5].wait()
+        loads[6].wait()
         for copy in rings:
             copy.wait_recv()
         away = off[0, 0, 0]
@@ -263,23 +292,32 @@
             + tiles[2].astype(F32) * here
         ).astype(BF)
 
-        @pl.loop(0, fx)
-        def _(q):
-            pre = jnp.dot(main[pl.ds(0, cells), :], ax[q], preferred_element_type=F32)
-            pre += jnp.dot(small[pl.ds(0, cells), :], yi[q], preferred_element_type=F32)
-            zb[0, q] = pre[:fy]
-            zb[1, q] = pre[cells - fy :]
-            phi = pre.astype(BF)
+        def dens(phi):
             psi = jnp.dot(phi, tile[...], preferred_element_type=F32)
-            den[pl.ds(q, 1), :] = rowsum(phi.astype(F32) * psi) * inv
-
+            return rowsum(phi.astype(F32) * psi) * inv
+
+        for q in range(fx):
+            den_in[pl.ds((q - 1) % fx, 1), :] = dens(phis[q])
+
+        def edge_cells(pre, at, width):
+            row = dens(pre.reshape(fx * width, slots).astype(BF))
+            for q in range(fx):
+                den_ed[pl.ds((q - 1) % fx, 1), pl.ds(at, width)] = row[:, q * width : (q + 1) * width]
+
+        def restore(value, at):
+            return jnp.dot(value, back[pl.ds(at, value.shape[1]), :].astype(F32),
+                           precision=lax.Precision.HIGHEST, preferred_element_type=F32)
+
+        edge_cells(edges[:, :y_rows], 0, y_rows)
+        placed = restore(den_in[...], 0)
         for key in (("ze", up), ("ze", dn), ("zl", up), ("zl", dn)):
             arrive(key)
-        for side in range(2):
-            pre = zb[side] + zi[side].astype(F32)
-            phi = pre.reshape(fx * fy, slots).astype(BF)
-            psi = jnp.dot(phi, tile[...], preferred_element_type=F32)
-            denb[pl.ds(side, 1), :] = rowsum(phi.astype(F32) * psi) * inv
+        pre = jnp.concatenate([
+            edges[:, y_rows : y_rows + fy] + zi[0].astype(F32),
+            edges[:, y_rows + fy : edge] + zi[1].astype(F32),
+        ], axis=1)
+        edge_cells(pre, y_rows, z_rows)
+        den[...] = placed + restore(den_ed[...], inner)
 
         for copy, axis, step in copies.values():
             pl.when(has(axis, step))(lambda copy=copy: copy.wait_send())
@@ -294,47 +332,47 @@
     fx, fy, fz = 2 * cx, 2 * cy, 2 * cz
     cells, rows = fy * fz, 4 * cy * cz
     scale = best_scale()
-    main, small = tables(cy, cz, scale)
-    anywhere = pl.BlockSpec(memory_space=pl.ANY)
+    main, small, back = tables(cy, cz, scale)
+    _, inner, y_rows, z_rows = cell_order(fy, fz)
+    anywhere = pl.BlockSpec(memory_space=pltpu.HBM)
     scalar = pl.BlockSpec(memory_space=pltpu.SMEM)
     vmem = pl.BlockSpec(memory_space=pltpu.VMEM)
-    den, denb = pl.pallas_call(
+    den = pl.pallas_call(
         make_kernel(cx, cy, cz, slots, scale),
-        out_shape=(
-            jax.ShapeDtypeStruct((fx, cells), F32),
-            jax.ShapeDtypeStruct((2, fx * fy), F32),
-        ),
-        in_specs=[anywhere, scalar, scalar, anywhere, anywhere, anywhere],
-        out_specs=(vmem, vmem),
+        out_shape=jax.ShapeDtypeStruct((fx, cells), F32),
+        in_specs=[anywhere, scalar, scalar, anywhere, anywhere, anywhere, anywhere],
+        out_specs=vmem,
         scratch_shapes=[
             pltpu.VMEM((bands, cx, cy * cz, slots), BF),
             pltpu.VMEM((fx, rows, slots), BF),
             pltpu.VMEM(main.shape, BF),
             pltpu.VMEM(small.shape, BF),
+            pltpu.VMEM(back.shape, BF),
             pltpu.VMEM((2, rows, slots), BF),
             pltpu.VMEM((2, rows, slots), BF),
             pltpu.VMEM((2, fx, 2 * cz, slots), BF),
             pltpu.VMEM((fx, 4 * cz, slots), BF),
             pltpu.VMEM((2, fx, fy, slots), BF),
             pltpu.VMEM((2, fx, fy, slots), BF),
-            pltpu.VMEM((2, fx, fy, slots), F32),
+            pltpu.VMEM((fx, inner, slots), BF),
+            pltpu.VMEM((fx, main.shape[0] - inner, slots), F32),
+            pltpu.VMEM((fx, inner), F32),
+            pltpu.VMEM((fx, y_rows + z_rows), F32),
             pltpu.VMEM((3, slots, slots), BF),
             pltpu.VMEM((slots, slots), BF),
-            pltpu.SemaphoreType.DMA((6,)),
+            pltpu.SemaphoreType.DMA((7,)),
             pltpu.SemaphoreType.DMA((12,)),
             pltpu.SemaphoreType.DMA((12,)),
         ],
         compiler_params=pltpu.CompilerParams(
-            collective_id=0, has_side_effects=True, vmem_limit_bytes=40 * 2**20
+            collective_id=0, has_side_effects=True, vmem_limit_bytes=63 * 2**20
         ),
     )(
         coefficients.reshape(bands, cx, cy * cz, slots),
         fun_count, tile_offset, kernel, jnp.asarray(main), jnp.asarray(small),
+        jnp.asarray(back),
     )
-    den = jnp.roll(den, -1, axis=0).reshape(fx, fz, fy)
-    faces = jnp.roll(denb.reshape(2, fx, fy), -1, axis=1)
-    den = jnp.concatenate([faces[0][:, None], den[:, 1:-1], faces[1][:, None]], axis=1)
-    return den.transpose(0, 2, 1).reshape(1, 1, 1, -1)
+    return den.reshape(1, 1, 1, -1)
 
 
 def solution(mesh):

time: 30.6 us -> 20.3 us (0.66)
  the two profiles are of different devices: /device:TPU:1 before, /device:TPU:9 now
where the time goes in v2:
time: 20.3 us; the launch traced here: 20.1 us
  Pallas kernels  17.4 us (86%)
  local copies, waits for them, and re-layouts  1.34 us (7%)
  between operations  1.3 us (6%)
    pallas_call x1, Pallas kernels, body(): pl.pallas_call(make_kernel(cx, cy, cz, slots, scale), out_shape=jax.Shape...  17.4 us
    reshape x1, local copies, waits for them, and re-layouts, body(): return den.reshape(1, 1, 1, -1)  1.34 us

profile of v2, /device:TPU:9, one launch (start us, length us, event | category | flops | bytes accessed | tf_op | source)
XLA Modules:
  0.0 20.1 jit_solution(8617629188014321620)
XLA Ops:
  1.3 17.4 %shard_map.73 = f32[16,256]{1,0:T(8,128)} custom-call(bf16[8,8,64,256]{3,2,1,0:T(8,128)(2,1)} %bitcast.1, s32[1,1,1]{2,1,0:T(1,128)S(6)} %copy.8.cnt, s32[1,1,1]{2,1,0:T(1,128)S(6)} %copy.9.off, bf16[1,256,256]{2,1,0:T(8,128)(2,1)} %ktile.1, bf16[288,256]{1,0:T(8,128)(2,1)} %constant.6.clone.main_h, bf16[96,32]{1,0:T(8,128)(2,1)} %constant.7.clone.small_h, ...), custom_call_target="tpu_custom_call" | custom-call | tf_op jit(solution)/shard_map/pallas_call | solution.py:340
  18.7 1.3 %reshape.7 = f32[1,1,1,4096]{3,2,1,0:T(1,128)} reshape(f32[16,256]{1,0:T(8,128)} %shard_map.73) | data formatting | bytes 32768 | tf_op jit(solution)/shard_map/reshape | solution.py:375

commit v3 on v2

--- a/solution.py
+++ b/solution.py
@@ -56,16 +56,17 @@
     halo[:, fy - 1, 1] = sz
     halo = halo.reshape(fy * fz, 4 * cz)[pick]
     send_z = np.zeros((2, fy, 2, 2, cy, cz))
-    send_zh = np.zeros((2, fy, 2, 2, cz))
+    send_zh = np.zeros((2, 2, 2, 2, cz))
     for c in range(2):
         for b in range(2):
             send_z[0, :, b, c, :, cz - 1] = sy[:, b] * BANDS[c][3]
             send_z[1, :, b, c, :, 0] = sy[:, b] * BANDS[c][0]
-        for side, row in ((0, 0), (1, fy - 1)):
-            send_zh[0, row, side, c, cz - 1] = BANDS[c][3]
-            send_zh[1, row, side, c, 0] = BANDS[c][0]
+        for side in range(2):
+            send_zh[0, side, side, c, cz - 1] = BANDS[c][3]
+            send_zh[1, side, side, c, 0] = BANDS[c][0]
     main = scale * np.concatenate([own, send_z.reshape(2 * fy, rows)], 0)
-    small = scale * np.concatenate([halo[inner:], send_zh.reshape(2 * fy, 4 * cz)], 0)
+    fill = np.zeros((12, 4 * cz))
+    small = scale * np.concatenate([halo[inner:], send_zh.reshape(4, 4 * cz), fill], 0)
     back = np.zeros((fy * fz, fy * fz))
     for at, (z, y) in enumerate(order):
         back[at, y * fz + z] = 1.0
@@ -88,7 +89,7 @@
     edge = y_rows + z_rows
 
     def kernel(coef, cnt, off, ktile, main_h, small_h, back_h, den,
-               cv, ax, main, small, back, xo, xi, yo, yi, zo, zi, phis, edges, den_in, den_ed,
+               cv, ax, main, small, back, xo, xi, yo, yi, zo, zi, zrow, zco, zci, phis, edges, den_in, den_ed,
                tiles, tile, lsem, ssem, rsem):
         ix, iy, iz = lax.axis_index("gx"), lax.axis_index("gy"), lax.axis_index("gz")
         gx, gy, gz = lax.axis_size("gx"), lax.axis_size("gy"), lax.axis_size("gz")
@@ -143,8 +144,13 @@
                 copies["z" + name, side] = (
                     remote(8 + 2 * part + side, zo.at[side, planes], zi.at[side, planes], "gz", iz + step),
                     "gz", step)
-        rings = [remote(2 + side, ktile.at[0], tiles.at[side], "gx", ring[step])
+            copies["zc", side] = (remote(14 + side, zco.at[side], zci.at[side], "gz", iz + step), "gz", step)
+        core = iy % 2
+        part = pl.ds(core * (slots // 2), slots // 2)
+        rings = [remote(2 + side, ktile.at[0, part], tiles.at[side, part], "gx", ring[step])
                  for side, step in ((up, 1), (dn, -1))]
+        passes = [remote(12 + side, tiles.at[side, part], tiles.at[side, part], "gy", iy + 1 - 2 * core)
+                  for side in (up, dn)]
 
         def start(key):
             copy, axis, step = copies[key]
@@ -173,10 +179,12 @@
         @pl.when(iz == 0)
         def _():
             zi[0] = jnp.zeros(zi.shape[1:], BF)
+            zci[0] = jnp.zeros(zci.shape[1:], BF)
 
         @pl.when(iz == gz - 1)
         def _():
             zi[1] = jnp.zeros(zi.shape[1:], BF)
+            zci[1] = jnp.zeros(zci.shape[1:], BF)
 
         live = jnp.where(
             lax.broadcasted_iota(jnp.int32, (1, slots), 1) < cnt[0, 0, 0], 1.0, 0.0
@@ -205,8 +213,6 @@
         pl.semaphore_wait(barrier, peers)
         start(("x", dn))
         start(("x", up))
-        for copy in rings:
-            copy.start()
 
         loads[2].wait()
 
@@ -235,16 +241,22 @@
 
         start(("ye", up))
         start(("ye", dn))
+        for copy in rings:
+            copy.start()
         loads[3].wait()
         loads[4].wait()
 
         def own_cells(q):
             pre = jnp.dot(main[...], ax[q], preferred_element_type=F32)
             phis[q] = pre[:inner].astype(BF)
-            edges[q] = pre[inner:]
+            edges[q] = pre[inner : cells]
+            zo[up, q] = pre[cells : cells + fy].astype(BF)
+            zo[dn, q] = pre[cells + fy :].astype(BF)
 
         for q in range(2, fx):
             own_cells(q)
+        start(("ze", up))
+        start(("ze", dn))
 
         arrive(("x", up))
         arrive(("x", dn))
@@ -258,30 +270,35 @@
         start(("yl", up))
         start(("yl", dn))
 
+        own_cells(0)
+        own_cells(1)
+        start(("zl", up))
+        start(("zl", dn))
+
         def y_halo(q):
-            pre = edges[q] + jnp.dot(small[...], yi[q], preferred_element_type=F32)
-            edges[q, :edge] = pre[:edge]
-            zo[up, q] = pre[edge : edge + fy].astype(BF)
-            zo[dn, q] = pre[edge + fy :].astype(BF)
+            add = jnp.dot(small[...], yi[q], preferred_element_type=F32)
+            edges[q] = edges[q] + add[:edge]
+            for row in range(4):
+                zrow[row // 2, pl.ds(row % 2 * fx + q, 1), :] = add[edge + row : edge + row + 1]
 
         arrive(("ye", up))
         arrive(("ye", dn))
         for q in range(2, fx):
             y_halo(q)
-        start(("ze", up))
-        start(("ze", dn))
-        own_cells(0)
-        own_cells(1)
         arrive(("yl", up))
         arrive(("yl", dn))
         y_halo(0)
         y_halo(1)
-        start(("zl", up))
-        start(("zl", dn))
-
+        zco[...] = zrow[...].astype(BF)
+        start(("zc", up))
+        start(("zc", dn))
+
+        for copy, onward in zip(rings, passes):
+            copy.wait_recv()
+            onward.start()
         loads[5].wait()
         loads[6].wait()
-        for copy in rings:
+        for copy in passes:
             copy.wait_recv()
         away = off[0, 0, 0]
         before = jnp.where(away == -1, 1.0, 0.0).astype(F32)
@@ -310,18 +327,24 @@
 
         edge_cells(edges[:, :y_rows], 0, y_rows)
         placed = restore(den_in[...], 0)
-        for key in (("ze", up), ("ze", dn), ("zl", up), ("zl", dn)):
-            arrive(key)
-        pre = jnp.concatenate([
-            edges[:, y_rows : y_rows + fy] + zi[0].astype(F32),
-            edges[:, y_rows + fy : edge] + zi[1].astype(F32),
-        ], axis=1)
+        for key in ("ze", "zl", "zc"):
+            arrive((key, up))
+            arrive((key, dn))
+        y_at = lax.broadcasted_iota(jnp.int32, (fx, fy, slots), 1)
+
+        def z_face(side):
+            late_rows = zci[side].astype(F32)
+            pre = edges[:, y_rows + side * fy : y_rows + (side + 1) * fy] + zi[side].astype(F32)
+            pre += jnp.where(y_at == 0, late_rows[:fx, None, :], 0.0)
+            return pre + jnp.where(y_at == fy - 1, late_rows[fx:, None, :], 0.0)
+
+        pre = jnp.concatenate([z_face(0), z_face(1)], axis=1)
         edge_cells(pre, y_rows, z_rows)
         den[...] = placed + restore(den_ed[...], inner)
 
         for copy, axis, step in copies.values():
             pl.when(has(axis, step))(lambda copy=copy: copy.wait_send())
-        for copy in rings:
+        for copy in rings + passes:
             copy.wait_send()
 
     return kernel
@@ -354,15 +377,18 @@
             pltpu.VMEM((fx, 4 * cz, slots), BF),
             pltpu.VMEM((2, fx, fy, slots), BF),
             pltpu.VMEM((2, fx, fy, slots), BF),
+            pltpu.VMEM((2, 2 * fx, slots), F32),
+            pltpu.VMEM((2, 2 * fx, slots), BF),
+            pltpu.VMEM((2, 2 * fx, slots), BF),
             pltpu.VMEM((fx, inner, slots), BF),
-            pltpu.VMEM((fx, main.shape[0] - inner, slots), F32),
+            pltpu.VMEM((fx, y_rows + z_rows, slots), F32),
             pltpu.VMEM((fx, inner), F32),
             pltpu.VMEM((fx, y_rows + z_rows), F32),
             pltpu.VMEM((3, slots, slots), BF),
             pltpu.VMEM((slots, slots), BF),
             pltpu.SemaphoreType.DMA((7,)),
-            pltpu.SemaphoreType.DMA((12,)),
-            pltpu.SemaphoreType.DMA((12,)),
+            pltpu.SemaphoreType.DMA((16,)),
+            pltpu.SemaphoreType.DMA((16,)),
         ],
         compiler_params=pltpu.CompilerParams(
             collective_id=0, has_side_effects=True, vmem_limit_bytes=63 * 2**20

time: 20.3 us -> 18.9 us (0.931)
  the two profiles are of different devices: /device:TPU:9 before, /device:TPU:1 now
where the time goes in v3:
time: 18.9 us; the launch traced here: 18.6 us
  Pallas kernels  16 us (85%)
  local copies, waits for them, and re-layouts  1.34 us (7%)
  between operations  1.3 us (7%)
    pallas_call x1, Pallas kernels, body(): pl.pallas_call(make_kernel(cx, cy, cz, slots, scale), out_shape=jax.Shape...  16 us
    reshape x1, local copies, waits for them, and re-layouts, body(): return den.reshape(1, 1, 1, -1)  1.34 us

profile of v3, /device:TPU:1, one launch (start us, length us, event | category | flops | bytes accessed | tf_op | source)
XLA Modules:
  0.0 18.6 jit_solution(2568390088390625153)
XLA Ops:
  1.3 16.0 %shard_map.73 = f32[16,256]{1,0:T(8,128)} custom-call(bf16[8,8,64,256]{3,2,1,0:T(8,128)(2,1)} %bitcast.1, s32[1,1,1]{2,1,0:T(1,128)S(6)} %copy.8.cnt, s32[1,1,1]{2,1,0:T(1,128)S(6)} %copy.9.off, bf16[1,256,256]{2,1,0:T(8,128)(2,1)} %ktile.1, bf16[288,256]{1,0:T(8,128)(2,1)} %constant.6.clone.main_h, bf16[80,32]{1,0:T(8,128)(2,1)} %constant.7.clone.small_h, ...), custom_call_target="tpu_custom_call" | custom-call | tf_op jit(solution)/shard_map/pallas_call | solution.py:363
  17.3 1.3 %reshape.7 = f32[1,1,1,4096]{3,2,1,0:T(1,128)} reshape(f32[16,256]{1,0:T(8,128)} %shard_map.73) | data formatting | bytes 32768 | tf_op jit(solution)/shard_map/reshape | solution.py:401

commit v4 on v3

--- a/solution.py
+++ b/solution.py
@@ -340,7 +340,9 @@
 
         pre = jnp.concatenate([z_face(0), z_face(1)], axis=1)
         edge_cells(pre, y_rows, z_rows)
-        den[...] = placed + restore(den_ed[...], inner)
+        flat = placed + restore(den_ed[...], inner)
+        for n in range(fx):
+            den[:, pl.ds(n * cells, cells)] = flat[n : n + 1]
 
         for copy, axis, step in copies.values():
             pl.when(has(axis, step))(lambda copy=copy: copy.wait_send())
@@ -362,7 +364,7 @@
     vmem = pl.BlockSpec(memory_space=pltpu.VMEM)
     den = pl.pallas_call(
         make_kernel(cx, cy, cz, slots, scale),
-        out_shape=jax.ShapeDtypeStruct((fx, cells), F32),
+        out_shape=jax.ShapeDtypeStruct((1, fx * cells), F32),
         in_specs=[anywhere, scalar, scalar, anywhere, anywhere, anywhere, anywhere],
         out_specs=vmem,
         scratch_shapes=[

time: 18.9 us -> 18.9 us (level)
    reshape x1 -> x0, local copies, waits for them, and re-layouts: 1.34 us -> none  [body(): return den.reshape(1, 1, 1, -1)]
    unnamed x0 -> x1, local copies, waits for them, and re-layouts: none -> 1.32 us
where the time goes in v4:
time: 18.9 us; the launch traced here: 18.6 us
  Pallas kernels  16 us (85%)
  local copies, waits for them, and re-layouts  1.32 us (7%)
  between operations  1.3 us (7%)
    pallas_call x1, Pallas kernels, body(): pl.pallas_call(make_kernel(cx, cy, cz, slots, scale), out_shape=jax.Shape...  16 us
    unnamed x1, local copies, waits for them, and re-layouts  1.32 us

profile of v4, /device:TPU:1, one launch (start us, length us, event | category | flops | bytes accessed | tf_op | source)
XLA Modules:
  0.0 18.6 jit_solution(1048142286172899828)
XLA Ops:
  1.3 16.0 %shard_map.73 = f32[1,4096]{1,0:T(1,128)} custom-call(bf16[8,8,64,256]{3,2,1,0:T(8,128)(2,1)} %bitcast.2, s32[1,1,1]{2,1,0:T(1,128)S(6)} %copy.9.cnt, s32[1,1,1]{2,1,0:T(1,128)S(6)} %copy.10.off, bf16[1,256,256]{2,1,0:T(8,128)(2,1)} %ktile.1, bf16[288,256]{1,0:T(8,128)(2,1)} %constant.6.clone.main_h, bf16[80,32]{1,0:T(8,128)(2,1)} %constant.7.clone.small_h, ...), custom_call_target="tpu_custom_call" | custom-call | tf_op jit(solution)/shard_map/pallas_call | solution.py:365
  17.3 1.3 %copy.11 = f32[1,1,1,4096]{3,2,1,0:T(1,128)} copy(f32[1,1,1,4096]{3,2,1,0:T(1,128)} %bitcast.3) | data formatting | bytes 32768
